TPU v7x, 32 devices: a whole 2x2x4 slice. The times are simulated.
32 devices in a mesh: hist: 4 (over z), rows: 8 (over y, x, core).
Axes of the slice: x: 2, y: 2, z: 4, core: 2. Of those that a mesh axis runs over, the one named last changes fastest.
Arguments:
- g_hist: bfloat16 [88, 64, 88, 128], P('hist', None, 'rows'), may hold values from -0.078125 to 0.078125
- g_last: float32 [64, 88, 128], P(None, 'rows'), may hold values from -6 to 6
- integral_last: float32 [64, 88, 128], P(None, 'rows'), may hold values from -6 to 6
- coupling: float32 [64, 64], replicated, may hold values from 0.5 to 2
- step_re: float32 [64, 64], replicated, may hold values from -1 to 2
- step_im: float32 [64, 64], replicated, may hold values from -0.375 to 0.375
Outputs:
- new_row: float32 [64, 88, 128], P('hist', 'rows')
- new_integral: float32 [64, 88, 128], P('hist', 'rows')
All inputs are finite; a program needn't handle non-finite values.
Results may differ from a plain program's by a relative error of at most 0.0055.
Values may be sent and summed in bfloat16 or wider, within the bound.
A program may use at most 64 MiB of HBM per device.

v0:
```python
import jax
import jax.numpy as jnp
from jax import lax
from jax.sharding import PartitionSpec as P

ITERS = 3


step_size = 0.5
half_step = 0.25


def broadcast(shard, axis, root):
    mine = lax.axis_index(axis) == root
    return lax.psum(jnp.where(mine, shard, jnp.zeros_like(shard)), axis)


def combine(first, second, width):
    return jnp.concatenate(
        [first[..., :width] - second[..., width:], first[..., width:] + second[..., :width]], -1
    )


def apply_step(step_re, step_im, field):
    orbits, times, wide = field.shape
    flat = field.reshape(orbits, times * wide)
    first = jnp.dot(
        step_re, flat, precision=lax.Precision.HIGHEST, preferred_element_type=jnp.float32
    ).reshape(orbits, times, wide)
    second = jnp.dot(
        step_im, flat, precision=lax.Precision.HIGHEST, preferred_element_type=jnp.float32
    ).reshape(orbits, times, wide)
    return combine(first, second, orbits)


def diag_power(field):
    count, times, wide = field.shape
    orbits = wide // 2
    mask = (jnp.arange(count)[:, None] == jnp.arange(orbits)[None, :]).astype(jnp.float32)
    real_part = field[..., :orbits]
    imag_part = field[..., orbits:]
    return jnp.sum((real_part * real_part + imag_part * imag_part) * mask[:, None, :])


def time_weights(first_time, count):
    moments = first_time + jnp.arange(count)
    return step_size * jnp.where(moments == 0, 0.5, 1.0).astype(jnp.float32)


def sigma_of(field, coupling, scale, weights):
    orbits = field.shape[0]
    real_part = field[..., :orbits]
    imag_part = field[..., orbits:]
    factor = (
        coupling[:, None, :]
        * (real_part * real_part + imag_part * imag_part)
        / scale
        * weights[None, :, None]
    )
    return jnp.concatenate([factor * real_part, factor * imag_part], -1).astype(jnp.bfloat16)


def on_device(g_hist, g_last, integral_last, coupling, step_re, step_im):
    orbits = g_last.shape[0]
    row_count = g_last.shape[1]
    wide = 2 * orbits
    hist_size = lax.axis_size("hist")
    rows_size = lax.axis_size("rows")
    fan_out = rows_size // hist_size
    hist_at = lax.axis_index("hist")
    total_cells = row_count * rows_size * orbits
    share = orbits // hist_size
    shifted = jnp.concatenate(
        [
            g_last[..., :orbits] + half_step * integral_last[..., orbits:],
            g_last[..., orbits:] - half_step * integral_last[..., :orbits],
        ],
        -1,
    )
    base = apply_step(step_re, step_im, shifted)
    history = g_hist.reshape(g_hist.shape[0] * orbits, row_count * wide)
    field = g_last
    part = lax.dynamic_slice_in_dim(g_last, hist_at * share, share, 0)
    integral_part = part
    for iteration in range(ITERS):
        power = lax.psum(diag_power(field), "rows")
        scale = 1.0 + power / total_cells
        accumulated = jnp.zeros((wide, row_count * wide), jnp.float32)
        for member in range(fan_out):
            root = fan_out * hist_at + member
            remote = broadcast(field, "rows", root)
            sigma_block = sigma_of(
                remote, coupling, scale, time_weights(root * row_count, row_count)
            )
            left_side = jnp.concatenate(
                [
                    sigma_block[..., :orbits].reshape(orbits, row_count * orbits),
                    sigma_block[..., orbits:].reshape(orbits, row_count * orbits),
                ],
                0,
            )
            block = lax.slice_in_dim(
                history, member * row_count * orbits, (member + 1) * row_count * orbits, axis=0
            )
            accumulated = accumulated + jnp.dot(
                left_side, block, preferred_element_type=jnp.float32
            )
        product = accumulated.reshape(wide, row_count, wide)
        terms = combine(product[:orbits], product[orbits:], orbits)
        integral = lax.psum(terms, "hist")
        field = base + jnp.concatenate(
            [half_step * integral[..., orbits:], -half_step * integral[..., :orbits]], -1
        )
        integral_part = lax.dynamic_slice_in_dim(integral, hist_at * share, share, 0)
        part = lax.dynamic_slice_in_dim(field, hist_at * share, share, 0)
    return (part, integral_part)


def solution(mesh):
    in_specs = (
        P("hist", None, "rows", None),
        P(None, "rows", None),
        P(None, "rows", None),
        P(),
        P(),
        P(),
    )
    out_specs = (P("hist", "rows", None), P("hist", "rows", None))
    return jax.shard_map(
        on_device, mesh=mesh, in_specs=in_specs, out_specs=out_specs, check_vma=False
    )
```

profile of v0, /device:TPU:0, one launch (start us, length us, event | category | flops | bytes accessed | tf_op | source)
XLA Modules:
  0.0 358.7 jit_solution(9746679796161743663)
XLA Ops:
  7.2 1.9 broadcast_select_fusion.4
  9.3 2.2 multiply_add_fusion
  11.4 15.9 %psum.85 = f32[]{:T(128)} all-reduce(f32[]{:T(128)} %get-tuple-element.58), channel_id=1, replica_groups=mesh['hist'=4,'rows'=8] {'rows'}, use_global_device_ids=true, to_apply=%region_2.3 | all-reduce | flops 1 | bytes 8 | tf_op jit(solution)/shard_map/psum | solution.py:86
  30.2 3.0 fusion.55
  33.3 3.1 copy.56
  38.6 2.4 fusion.66
  41.0 28.4 %all-reduce.20.cloned.1.call-done = (f32[64,11,128]{2,0,1:T(8,128)}, f32[64,11,128]{2,0,1:T(8,128)}) async-done(((f32[64,11,128]{2,0,1:T(8,128)}, f32[64,11,128]{2,0,1:T(8,128)}), (f32[64,11,128]{2,0,1:T(8,128)}, f32[64,11,128]{2,0,1:T(8,128)})) %all-reduce.20.cloned.1.call-update) | async-done | bytes 720912 | tf_op jit(solution)/shard_map/psum | solution.py:15
  69.4 2.3 multiply_convert_fusion.9
  71.7 1.7 copy.54
  78.7 1.8 slice.237
  87.2 2.4 copy_add_fusion.3
  89.5 32.1 %all-reduce.10.cloned.1.call-done = f32[64,11,128]{2,0,1:T(8,128)} async-done(((f32[64,11,128]{2,0,1:T(8,128)}), f32[64,11,128]{2,0,1:T(8,128)}) %all-reduce.10.cloned.1.call-update) | async-done | bytes 360464 | tf_op jit(solution)/shard_map/psum | solution.py:110
  122.9 2.0 broadcast_select_fusion.2
  126.4 1.9 fusion.22
  128.3 13.0 %psum.89 = f32[]{:T(128)} all-reduce(f32[]{:T(128)} %fusion.22), channel_id=1, replica_groups=mesh['hist'=4,'rows'=8] {'rows'}, use_global_device_ids=true, to_apply=%region_7.8 | all-reduce | flops 1 | bytes 8 | tf_op jit(solution)/shard_map/psum | solution.py:86
  142.0 39.8 %all-reduce.18.cloned.1.call-done = (f32[64,11,128]{2,0,1:T(8,128)}, f32[64,11,128]{2,0,1:T(8,128)}) async-done(((f32[64,11,128]{2,0,1:T(8,128)}, f32[64,11,128]{2,0,1:T(8,128)}), (f32[64,11,128]{2,0,1:T(8,128)}, f32[64,11,128]{2,0,1:T(8,128)})) %all-reduce.18.cloned.1.call-update) | async-done | bytes 720912 | tf_op jit(solution)/shard_map/psum | solution.py:15
  181.8 2.5 multiply_convert_fusion.5
  186.0 1.7 copy.64
  187.7 1.7 copy.62
  190.2 1.8 fusion.5
  194.6 1.8 slice.257
  196.4 1.8 slice.260
  202.5 35.9 %all-reduce.12.cloned.1.call-done = f32[64,11,128]{2,0,1:T(8,128)} async-done(((f32[64,11,128]{2,0,1:T(8,128)}), f32[64,11,128]{2,0,1:T(8,128)}) %all-reduce.12.cloned.1.call-update) | async-done | bytes 360464 | tf_op jit(solution)/shard_map/psum | solution.py:110
  239.6 2.0 broadcast_select_fusion
  243.2 1.9 fusion.19
  245.1 12.8 %psum.93 = f32[]{:T(128)} all-reduce(f32[]{:T(128)} %fusion.19), channel_id=1, replica_groups=mesh['hist'=4,'rows'=8] {'rows'}, use_global_device_ids=true, to_apply=%region_12.13 | all-reduce | flops 1 | bytes 8 | tf_op jit(solution)/shard_map/psum | solution.py:86
  258.5 40.0 %all-reduce.16.cloned.1.call-done = (f32[64,11,128]{2,0,1:T(8,128)}, f32[64,11,128]{2,0,1:T(8,128)}) async-done(((f32[64,11,128]{2,0,1:T(8,128)}, f32[64,11,128]{2,0,1:T(8,128)}), (f32[64,11,128]{2,0,1:T(8,128)}, f32[64,11,128]{2,0,1:T(8,128)})) %all-reduce.16.cloned.1.call-update) | async-done | bytes 720912 | tf_op jit(solution)/shard_map/psum | solution.py:15
  298.5 2.5 multiply_convert_fusion.1
  302.7 1.7 copy.72
  304.4 1.7 copy.70
  306.9 1.8 fusion.3
  312.4 35.9 %all-reduce.14.cloned.1.call-done = f32[64,11,128]{2,0,1:T(8,128)} async-done(((f32[64,11,128]{2,0,1:T(8,128)}), f32[64,11,128]{2,0,1:T(8,128)}) %all-reduce.14.cloned.1.call-update) | async-done | bytes 360464 | tf_op jit(solution)/shard_map/psum | solution.py:110
  (83 shorter events, 41.1 us)
Async XLA Ops:
  7.2 20.1 %copy-start = (f32[64,64]{1,0:T(8,128)S(1)}, f32[64,64]{1,0:T(8,128)}, u32[]{:S(2)}) copy-start(f32[64,64]{1,0:T(8,128)} %param.11) | copy-start | bytes 49156
  7.2 20.7 %copy-start.11 = (f32[64,64]{1,0:T(8,128)S(1)}, f32[64,64]{1,0:T(8,128)}, u32[]{:S(2)}) copy-start(f32[64,64]{1,0:T(8,128)} %param.10) | copy-start | bytes 49156
  7.2 62.2 %all-reduce.20.cloned.1.call-start = ((), (), s32[]{:S(2)}) async-start(), calls=%async_computation.5 | async-start | bytes 1441792 | tf_op jit(solution)/shard_map/psum | solution.py:15
  9.2 112.4 %all-reduce.10.cloned.1.call-start = ((), (), s32[]{:S(2)}) async-start(), calls=%async_computation | async-start | bytes 720896 | tf_op jit(solution)/shard_map/psum | solution.py:110
  36.4 33.0 %copy-start.10 = (f32[64,64]{1,0:T(8,128)S(1)}, f32[64,64]{1,0:T(8,128)}, u32[]{:S(2)}) copy-start(f32[64,64]{1,0:T(8,128)} %param.9) | copy-start | bytes 49156
  74.6 1.8 copy-start.1
  74.6 1.8 copy-start.8
  85.7 96.1 %all-reduce.18.cloned.1.call-start = ((), (), s32[]{:S(2)}) async-start(), calls=%async_computation.4 | async-start | bytes 1441792 | tf_op jit(solution)/shard_map/psum | solution.py:15
  124.8 0.7 copy-start.6
  126.4 112.0 %all-reduce.12.cloned.1.call-start = ((), (), s32[]{:S(2)}) async-start(), calls=%async_computation.1 | async-start | bytes 720896 | tf_op jit(solution)/shard_map/psum | solution.py:110
  190.2 2.0 copy-start.2
  190.2 2.0 copy-start.9
  202.5 96.1 %all-reduce.16.cloned.1.call-start = ((), (), s32[]{:S(2)}) async-start(), calls=%async_computation.3 | async-start | bytes 1441792 | tf_op jit(solution)/shard_map/psum | solution.py:15
  241.6 0.7 copy-start.5
  243.1 105.1 %all-reduce.14.cloned.1.call-start = ((), (), s32[]{:S(2)}) async-start(), calls=%async_computation.2 | async-start | bytes 720896 | tf_op jit(solution)/shard_map/psum | solution.py:110
  306.9 2.0 copy-start.3
  306.9 2.0 copy-start.7
  311.0 38.5 %copy-start.4 = (f32[64,11,64]{2,0,1:T(8,128)S(1)}, f32[64,11,64]{2,0,1:T(8,128)}, u32[]{:S(2)}) copy-start(f32[64,11,64]{2,0,1:T(8,128)} %get-tuple-element.70) | copy-start | bytes 540676
Sparse Core Ops, SparseCore 0:
  11.2 58.1 all-reduce.19
  85.8 35.7 all-reduce.9
  126.5 55.2 all-reduce.17
  202.6 35.7 all-reduce.11
  243.3 55.2 all-reduce.15
  312.5 35.7 all-reduce.13
where the time goes:
time: 360 us; the launch traced here: 359 us
  waiting for transfers between devices  212 us (59%)
  local copies, waits for them, and re-layouts  46.8 us (13%)
  blocking collectives  41.7 us (12%)
  other arithmetic  31.5 us (9%)
  between operations  16.3 us (5%)
  matrix products  9.93 us (3%)
    psum x3, waiting for transfers between devices, broadcast(): return lax.psum(jnp.where(mine, shard, jnp.zeros_like(shard)), axis)  108 us
    psum x3, waiting for transfers between devices, on_device(): integral = lax.psum(terms, 'hist')  104 us
    psum x3, blocking collectives, on_device(): power = lax.psum(diag_power(field), 'rows')  41.7 us
    dot_general x6, matrix products, on_device(): jnp.dot(left_side, block, preferred_element_type=jnp.float32)  8.78 us
    slice x9, local copies, waits for them, and re-layouts, on_device(): terms = combine(product[:orbits], product[orbits:], orbits)  8.31 us
    slice x6, local copies, waits for them, and re-layouts, on_device(): sigma_block[..., orbits:].reshape(orbits, row_count * orbits)  7.79 us
    slice x3, local copies, waits for them, and re-layouts, on_device(): lax.slice_in_dim(history, member * row_count * orbits, (member + 1) * row...  7.75 us
    select_n x5, other arithmetic, broadcast(): return lax.psum(jnp.where(mine, shard, jnp.zeros_like(shard)), axis)  7.41 us
  transfers between devices with their start and end apart: 6, of which 6 were waited for; matrix products, arithmetic and copies ran while one was open for 6% of the time, Pallas kernels for 0%

commit v1 on v0

v1 whole, which is shorter than its diff:
```python
import functools

import jax
import jax.numpy as jnp
from jax import lax
from jax.experimental import pallas as pl
from jax.experimental.pallas import tpu as pltpu
from jax.sharding import PartitionSpec as P

ITERS = 3
GROUP = 4
HALF = 0.25
STEP = 0.5
MESH = pl.DeviceIdType.MESH


def kernel(
    hist, rows, count, orbits, share, tall,
    g_ref, gl_ref, il_ref, coup_ref, re_ref, im_ref,
    row_ref, int_ref,
    ghist, ebuf, lbuf, dbuf, base, tbuf, tsend, trecv, dacc, pcol, prow, inv_ref,
    gsem, esend, lrecv, osend, orecv, ssend, srecv, csend, crecv, wsend, wrecv,
):
    wide = 2 * orbits
    groups = -(-count // GROUP)
    chips = rows // 2
    cells = float(count * rows * orbits)
    mark_at = 4 * tall
    h = lax.axis_index("hist")
    r = lax.axis_index("rows")
    q = r // 2
    k = r % 2
    other = 1 - k
    partner = r + 1 - 2 * k
    home = h == q
    away = jnp.logical_not(home)
    mine = pl.ds(pl.multiple_of(h * share, share), tall)

    loading = pltpu.make_async_copy(g_ref, ghist, gsem)
    loading.start()

    def sizes(g):
        return min(GROUP, count - g * GROUP)

    def loop(low, high, body):
        def step(o, c):
            body(o)
            return c

        lax.fori_loop(low, high, step, 0)

    barrier = pltpu.get_barrier_semaphore()

    def greet(hh, rr):
        pl.semaphore_signal(barrier, inc=1, device_id=(hh, rr), device_id_type=MESH)

    loop(1, hist, lambda o: greet((h + o) % hist, r))
    loop(1, rows, lambda o: greet(h, (r + o) % rows))

    @pl.when(away)
    def _():
        loop(1, hist, lambda o: greet((h + o) % hist, 2 * h + k))

    near = hist - 1 + rows - 1
    lane = lax.broadcasted_iota(jnp.int32, (tall, wide), 1)
    line = lax.broadcasted_iota(jnp.int32, (tall, wide), 0)
    low = lane < orbits
    minus_plus = jnp.where(low, -1.0, 1.0).astype(jnp.float32)
    here = line + h * share
    diagonal = (line < share) & ((lane == here) | (lane == here + orbits))
    eye = jnp.where(diagonal, 1.0, 0.0).astype(jnp.float32)
    coup_rows = coup_ref[mine, :]
    coup = jnp.concatenate([coup_rows, coup_rows], 1)

    def turn(x):
        return pltpu.roll(x, orbits, 1)

    def joined(first, second):
        return first + minus_plus * turn(second)

    def sigma_copy(it, g, o):
        target = (q + o) % chips
        return pltpu.make_async_remote_copy(
            src_ref=ebuf.at[it, g],
            dst_ref=lbuf.at[it, k, g, h],
            send_sem=esend.at[it, g, o],
            recv_sem=lrecv.at[it, g, h],
            device_id=(q, 2 * target + k),
            device_id_type=MESH,
        )

    def sigma_from(it, g, source):
        return pltpu.make_async_remote_copy(
            src_ref=ebuf.at[it, g],
            dst_ref=lbuf.at[it, k, g, source],
            send_sem=esend.at[it, g, 0],
            recv_sem=lrecv.at[it, g, source],
            device_id=(source, 2 * h + k),
            device_id_type=MESH,
        )

    def pair_copy(it, g, member):
        return pltpu.make_async_remote_copy(
            src_ref=lbuf.at[it, member, g],
            dst_ref=lbuf.at[it, member, g],
            send_sem=osend.at[it, g],
            recv_sem=orecv.at[it, g],
            device_id=(h, partner),
            device_id_type=MESH,
        )

    def column_copy(it, o):
        return pltpu.make_async_remote_copy(
            src_ref=pcol.at[it, h],
            dst_ref=pcol.at[it, h],
            send_sem=csend.at[it, o],
            recv_sem=crecv.at[it, h],
            device_id=((h + o) % hist, r),
            device_id_type=MESH,
        )

    def column_from(it, source):
        return pltpu.make_async_remote_copy(
            src_ref=pcol.at[it, source],
            dst_ref=pcol.at[it, source],
            send_sem=csend.at[it, 0],
            recv_sem=crecv.at[it, source],
            device_id=(source, r),
            device_id_type=MESH,
        )

    def plane_copy(it, o):
        return pltpu.make_async_remote_copy(
            src_ref=prow.at[it, r],
            dst_ref=prow.at[it, r],
            send_sem=wsend.at[it, o],
            recv_sem=wrecv.at[it, r],
            device_id=(h, (r + o) % rows),
            device_id_type=MESH,
        )

    def plane_from(it, source):
        return pltpu.make_async_remote_copy(
            src_ref=prow.at[it, source],
            dst_ref=prow.at[it, source],
            send_sem=wsend.at[it, 0],
            recv_sem=wrecv.at[it, source],
            device_id=(h, source),
            device_id_type=MESH,
        )

    def terms_copy(it, g, target, source):
        times = pl.ds(g * GROUP, sizes(g))
        return pltpu.make_async_remote_copy(
            src_ref=tsend.at[it, target, times],
            dst_ref=trecv.at[it, source, times],
            send_sem=ssend.at[it, g, target],
            recv_sem=srecv.at[it, g, source],
            device_id=(target, r),
            device_id_type=MESH,
        )

    def make_sigma(it, g, fields):
        norms = []
        total = jnp.zeros((tall, wide), jnp.float32)
        for f in fields:
            sq = f * f
            n2 = sq + turn(sq)
            norms.append(n2)
            total = total + n2 * (1.0 / (GROUP * tall * wide))
        mean = 1.0 + jnp.sum(total, keepdims=True)
        mark = jnp.broadcast_to(mean, (16, wide)).astype(jnp.bfloat16)
        inverse = 1.0 / mark.astype(jnp.float32)[0:1, :]
        taus = []
        for i, f in enumerate(fields):
            weight = STEP
            if g == 0 and i == 0:
                weight = jnp.where(r == 0, 0.5 * STEP, STEP).astype(jnp.float32)
            taus.append(norms[i] * (inverse * weight) * coup * f)
        while len(taus) < GROUP:
            taus.append(jnp.zeros((tall, wide), jnp.float32))
        parts = []
        for p in range(GROUP // 2):
            a, b = taus[2 * p], taus[2 * p + 1]
            parts.append(jnp.where(low, a, turn(b)).astype(jnp.bfloat16))
            parts.append(jnp.where(low, turn(a), b).astype(jnp.bfloat16))
        for i, part in enumerate(parts):
            ebuf[it, g, pl.ds(i * tall, tall), :] = part
        ebuf[it, g, pl.ds(mark_at, 16), :] = mark

        @pl.when(home)
        def _():
            for i, part in enumerate(parts):
                lbuf[it, k, g, h, pl.ds(i * tall, tall), :] = part
            lbuf[it, k, g, h, pl.ds(mark_at, 16), :] = mark

    def send_sigma(it, g):
        loop(1, chips, lambda o: sigma_copy(it, g, o).start())

        @pl.when(away)
        def _():
            sigma_copy(it, g, 0).start()

    def send_power(it):
        pcol[it, h] = jnp.broadcast_to(jnp.sum(dacc[...], keepdims=True), (8, wide))
        loop(1, hist, lambda o: column_copy(it, o).start())

    def pass_power(it):
        loop(1, hist, lambda o: column_from(it, (h + o) % hist).wait_recv())
        prow[it, r] = jnp.sum(pcol[it], axis=0)
        loop(1, rows, lambda o: plane_copy(it, o).start())

    def take_scale(it):
        loop(1, rows, lambda o: plane_from(it, (r + o) % rows).wait_recv())
        inv_ref[...] = 1.0 / (1.0 + jnp.sum(prow[it], axis=0) * (1.0 / cells))

    dacc[...] = jnp.zeros((tall, wide), jnp.float32)
    for g in range(groups):
        fields = [gl_ref[g * GROUP + i, mine, :] for i in range(sizes(g))]
        for f in fields:
            dacc[...] += f * f * eye
        make_sigma(0, g, fields)

    @pl.when(away)
    def _():
        pl.semaphore_wait(barrier, near + chips - 1)

    @pl.when(home)
    def _():
        pl.semaphore_wait(barrier, near)

    for g in range(groups):
        send_sigma(0, g)
    send_power(0)

    step = jnp.concatenate([re_ref[mine, :], im_ref[mine, :]], 0)
    whole_sign = jnp.where(
        lax.broadcasted_iota(jnp.int32, (orbits, wide), 1) < orbits, HALF, -HALF
    ).astype(jnp.float32)
    for t in range(count):
        shifted = gl_ref[t, pl.ds(0, orbits), :] + whole_sign * turn(il_ref[t])
        both = jnp.dot(
            step, shifted, precision=lax.Precision.HIGHEST,
            preferred_element_type=jnp.float32,
        )
        base[t] = joined(both[:tall], both[tall:])

    def multiply_pair(it, member, j, place, t):
        left = jnp.concatenate(
            [
                jnp.concatenate(
                    [
                        lbuf[it, member, j, s, pl.ds(2 * p * tall, 2 * tall), :]
                        for s in range(hist)
                    ],
                    0,
                )
                for p in range(GROUP // 2)
            ],
            1,
        )[:, :sizes(j) * orbits]
        first = member * count + j * GROUP
        pair = range(t, min(t + 2, count))
        right = jnp.concatenate(
            [
                jnp.concatenate([ghist[first + i, u] for i in range(sizes(j))], 0)
                for u in pair
            ],
            1,
        )
        dbuf[place, j, :, t * wide:(t + len(pair)) * wide] = jnp.dot(
            left, right, preferred_element_type=jnp.float32
        )

    def multiply(it, member, j, place):
        for t in range(0, count, 2):
            multiply_pair(it, member, j, place, t)

    def iteration(it, c):
        pass_power(it)
        for j in range(groups):
            @pl.when(away)
            def _():
                sigma_from(it, j, h).wait_recv()

            loop(1, hist, lambda o: sigma_from(it, j, (h + o) % hist).wait_recv())
            pair_copy(it, j, k).start()

            if j == 0:
                @pl.when(it == 0)
                def _():
                    loading.wait()
            if j > 0:
                pair_copy(it, j - 1, other).wait_recv()
                multiply(it, other, j - 1, 1)
            multiply(it, k, j, 0)
        take_scale(it)
        pair_copy(it, groups - 1, other).wait_recv()

        inv = inv_ref[0:1, :]
        facs = []
        for s in range(hist):
            for place, member in ((0, k), (1, other)):
                for j in range(groups):
                    mark = lbuf[it, member, j, s, pl.ds(mark_at, 16), :].astype(jnp.float32)
                    facs.append((s, place, j, mark[0:1, :] * inv))
        for g in range(groups):
            for t in range(g * GROUP, g * GROUP + sizes(g)):
                if t % 2 == 0:
                    multiply_pair(it, other, groups - 1, 1, t)
                for s in range(hist):
                    product = None
                    for at, place, j, fac in facs:
                        if at == s:
                            piece = dbuf[
                                place, j, 2 * tall * s:2 * tall * (s + 1),
                                t * wide:(t + 1) * wide,
                            ] * fac
                            product = piece if product is None else product + piece
                    value = joined(product[:tall], product[tall:])
                    tbuf[s, t] = value
                    tsend[it, s, t] = value.astype(jnp.bfloat16)
            loop(1, hist, lambda o: terms_copy(it, g, (h + o) % hist, h).start())

        dacc[...] = jnp.zeros((tall, wide), jnp.float32)
        for g in range(groups):
            span = range(g * GROUP, g * GROUP + sizes(g))

            def add(o):
                source = (h + o) % hist
                terms_copy(it, g, source, source).wait_recv()
                for t in span:
                    tbuf[h, t] += trecv[it, source, t].astype(jnp.float32)

            loop(1, hist, add)
            fields = []
            for t in span:
                total = tbuf[h, t]
                f = base[t] - (HALF * minus_plus) * turn(total)
                dacc[...] += f * f * eye
                fields.append(f)

            @pl.when(it == ITERS - 1)
            def _():
                for i, t in enumerate(span):
                    int_ref[t] = tbuf[h, t][:share]
                    row_ref[t] = fields[i][:share]

            @pl.when(it < ITERS - 1)
            def _():
                make_sigma(it + 1, g, fields)
                send_sigma(it + 1, g)
                if g == groups - 1:
                    send_power(it + 1)

        for g in range(groups):
            loop(1, chips, lambda o: sigma_copy(it, g, o).wait_send())

            @pl.when(away)
            def _():
                sigma_copy(it, g, 0).wait_send()

            pair_copy(it, g, k).wait_send()
            loop(1, hist, lambda o: terms_copy(it, g, (h + o) % hist, h).wait_send())
        loop(1, hist, lambda o: column_copy(it, o).wait_send())
        loop(1, rows, lambda o: plane_copy(it, o).wait_send())
        return c

    lax.fori_loop(0, ITERS, iteration, 0)


def on_device(g_hist, g_last, integral_last, coupling, step_re, step_im):
    orbits, count, wide = g_last.shape
    hist = lax.axis_size("hist")
    rows = lax.axis_size("rows")
    assert rows == 2 * hist and g_hist.shape[0] == 2 * count
    groups = -(-count // GROUP)
    share = orbits // hist
    tall = -(-share // 16) * 16
    columns = count * wide
    history_shape = (g_hist.shape[0], count, orbits, wide)
    history = g_hist.transpose(0, 2, 1, 3)
    field = g_last.transpose(1, 0, 2)
    before = integral_last.transpose(1, 0, 2)
    if tall > share:
        extra = tall - share
        field = jnp.pad(field, ((0, 0), (0, extra), (0, 0)))
        coupling = jnp.pad(coupling, ((0, extra), (0, 0)))
        step_re = jnp.pad(step_re, ((0, extra), (0, 0)))
        step_im = jnp.pad(step_im, ((0, extra), (0, 0)))
    dma = pltpu.SemaphoreType.DMA
    part = jax.ShapeDtypeStruct((count, share, wide), jnp.float32)
    chunk = 4 * tall + 16
    row, integral = pl.pallas_call(
        functools.partial(kernel, hist, rows, count, orbits, share, tall),
        out_shape=(part, part),
        in_specs=[pl.BlockSpec(memory_space=pl.ANY)]
        + [pl.BlockSpec(memory_space=pltpu.VMEM)] * 5,
        out_specs=(pl.BlockSpec(memory_space=pltpu.VMEM),) * 2,
        scratch_shapes=[
            pltpu.VMEM(history_shape, jnp.bfloat16),
            pltpu.VMEM((ITERS, groups, chunk, wide), jnp.bfloat16),
            pltpu.VMEM((ITERS, 2, groups, hist, chunk, wide), jnp.bfloat16),
            pltpu.VMEM((2, groups, 2 * tall * hist, columns), jnp.float32),
            pltpu.VMEM((count, tall, wide), jnp.float32),
            pltpu.VMEM((hist, count, tall, wide), jnp.float32),
            pltpu.VMEM((ITERS, hist, count, tall, wide), jnp.bfloat16),
            pltpu.VMEM((ITERS, hist, count, tall, wide), jnp.bfloat16),
            pltpu.VMEM((tall, wide), jnp.float32),
            pltpu.VMEM((ITERS, hist, 8, wide), jnp.float32),
            pltpu.VMEM((ITERS, rows, 8, wide), jnp.float32),
            pltpu.VMEM((8, wide), jnp.float32),
            dma,
            dma((ITERS, groups, rows // 2)),
            dma((ITERS, groups, hist)),
            dma((ITERS, groups)),
            dma((ITERS, groups)),
            dma((ITERS, groups, hist)),
            dma((ITERS, groups, hist)),
            dma((ITERS, hist)),
            dma((ITERS, hist)),
            dma((ITERS, rows)),
            dma((ITERS, rows)),
        ],
        compiler_params=pltpu.CompilerParams(
            collective_id=0, has_side_effects=True, vmem_limit_bytes=60 * 1024 * 1024
        ),
        cost_estimate=pl.CostEstimate(
            flops=ITERS * 4 * wide * count * orbits * columns,
            bytes_accessed=4 * count * orbits * columns,
            transcendentals=0,
        ),
        name="memory_steps",
    )(history, field, before, coupling, step_re, step_im)
    return (row.transpose(1, 0, 2), integral.transpose(1, 0, 2))


def solution(mesh):
    in_specs = (
        P("hist", None, "rows", None),
        P(None, "rows", None),
        P(None, "rows", None),
        P(),
        P(),
        P(),
    )
    out_specs = (P("hist", "rows", None), P("hist", "rows", None))
    return jax.shard_map(
        on_device, mesh=mesh, in_specs=in_specs, out_specs=out_specs, check_vma=False
    )
```

time: 360 us -> 90.3 us (0.25)
  waiting for transfers between devices: 212 us -> 0 us
  Pallas kernels: 0 us -> 86.4 us
  local copies, waits for them, and re-layouts: 46.8 us -> 3.07 us
  blocking collectives: 41.7 us -> 0 us
  other arithmetic: 31.5 us -> 0 us
  between operations: 16.3 us -> 0.64 us
  matrix products: 9.93 us -> 0 us
    psum x6 -> x0, waiting for transfers between devices: 212 us -> none  [the longest x3 108 us: broadcast(): return lax.psum(jnp.where(mine, shard, jnp.zeros_like(shard)), axis)]
    pallas_call x0 -> x1, Pallas kernels: none -> 86.4 us  [on_device(): pl.pallas_call(functools.partial(kernel, hist, rows, count, orbits, share...]
    psum x3 -> x0, blocking collectives: 41.7 us -> none  [on_device(): power = lax.psum(diag_power(field), 'rows')]
    slice x32 -> x0, local copies, waits for them, and re-layouts: 40.5 us -> none  [the longest x9 8.31 us: on_device(): terms = combine(product[:orbits], product[orbits:], orbits)]
    dot_general x8 -> x0, matrix products: 9.93 us -> none  [the longest x6 8.78 us: on_device(): jnp.dot(left_side, block, preferred_element_type=jnp.float32)]
    select_n x5 -> x0, other arithmetic: 7.41 us -> none  [broadcast(): return lax.psum(jnp.where(mine, shard, jnp.zeros_like(shard)), axis)]
    slice x3 -> x0, other arithmetic: 7.25 us -> none  [on_device(): sigma_block[..., :orbits].reshape(orbits, row_count * orbits)]
    add x6 -> x0, other arithmetic: 5.95 us -> none  [the longest x4 3.02 us: combine(): first[..., width:] + second[..., :width]]
  transfers between devices with their start and end apart: 6 -> 0, of which waited for: 6 -> 0; matrix products, arithmetic and copies ran while one was open for 6% -> 0% of each run, Pallas kernels for 0% -> 0%
where the time goes in v1:
time: 90.3 us; the launch traced here: 90.1 us
  Pallas kernels  86.4 us (96%)
  local copies, waits for them, and re-layouts  3.07 us (3%)
    pallas_call x1, Pallas kernels, on_device(): pl.pallas_call(functools.partial(kernel, hist, rows, count, orbits, share...  86.4 us
    unnamed x2, local copies, waits for them, and re-layouts  3.07 us

profile of v1, /device:TPU:0, one launch (start us, length us, event | category | flops | bytes accessed | tf_op | source)
XLA Modules:
  0.0 90.1 jit_solution(2038494093860120044)
XLA Ops:
  0.6 86.4 %memory_steps.1 = (f32[11,16,128]{2,1,0:T(8,128)}, f32[11,16,128]{2,1,0:T(8,128)}) custom-call(bf16[22,11,64,128]{3,2,1,0:T(8,128)(2,1)} %bitcast.7, f32[11,64,128]{2,1,0:T(8,128)} %bitcast.8, f32[11,64,128]{2,1,0:T(8,128)} %bitcast.9, f32[64,64]{1,0:T(8,128)} %coup_ref.1, f32[64,64]{1,0:T(8,128)} %re_ref.1, f32[64,64]{1,0:T(8,128)} %im_ref.1), custom_call_target="tpu_custom_call" | custom-call | flops 1522532352 | bytes 3964928 | tf_op jit(solution)/shard_map/memory_steps/pallas_call | solution.py:394
  87.1 1.5 %copy.10 = f32[16,11,128]{2,0,1:T(8,128)} copy(f32[16,11,128]{2,0,1:T(8,128)} %bitcast.6) | data formatting | bytes 180224
  88.6 1.5 %copy.11 = f32[16,11,128]{2,0,1:T(8,128)} copy(f32[16,11,128]{2,0,1:T(8,128)} %bitcast.5) | data formatting | bytes 180224
